TPU v7x, 128 devices: a whole 4x4x4 slice. The times are simulated.
128 devices in a mesh: leaf: 8 (over x, core), sub: 16 (over z, y).
Axes of the slice: x: 4, y: 4, z: 4, core: 2. Of those that a mesh axis runs over, the one named last changes fastest.
Arguments:
- points: bfloat16 [524288, 128], P(('leaf', 'sub')), may hold values from -5 to 5
- charges: bfloat16 [524288, 64], P(('leaf', 'sub')), may hold values from -0.796875 to 0.796875
- near_leaves: int32 [1024, 12], P(('leaf', 'sub')), may hold values from 0 to 1023, as said below
- leaf_interpolant: bfloat16 [1024, 512, 256], P(('leaf', 'sub')), may hold values from -0.25 to 0.25
- skel_leaf: int32 [1024, 256], P(('leaf', 'sub')), may hold values from 0 to 511, as said below
- interp_mid: bfloat16 [128, 2048, 256], P(('leaf', 'sub')), may hold values from -0.375 to 0.375
- skel_mid: int32 [128, 256], P(('leaf', 'sub')), may hold values from 0 to 2047, as said below
- mid_partners: int32 [128, 4], P(('leaf', 'sub')), may hold values from 0 to 127, as said below
- interp_top: bfloat16 [8, 4096, 256], P('leaf', 'sub'), may hold values from -0.09375 to 0.09375
- skel_top: int32 [8, 256], P('leaf'), may hold values from 0 to 4095, as said below
Outputs:
- potential: float32 [524288, 64], P(('leaf', 'sub'))
Inputs may be any that keep to these rules, and one draw needn't show every extreme that they name: `near_leaves`: row l lists leaf l first, then 12 - 1 other different leaves of the same top node. Over the rows of one device's 8 leaves, at most 2 different leaves of any one other device are named. `skel_leaf`: different indices in a row. `skel_mid`: different indices in a row. `skel_top`: different indices in a row. `mid_partners`: different middle nodes of the same top node, never the node itself.
All inputs are finite; a program needn't handle non-finite values.
Results may differ from a plain program's by a relative error of at most 0.008.
Values may be sent and summed in bfloat16 or wider, within the bound.
A program may use at most 128 MiB of HBM per device.

v0:
```python
import jax
import jax.numpy as jnp
from jax import lax
from jax.sharding import PartitionSpec as P

CAP = 2


kernel_rate = 0.25


def laid_out(tiles, dim):
    tiles = jnp.moveaxis(tiles, 0, dim)
    dims = tiles.shape
    return tiles.reshape(*dims[:dim], dims[dim] * dims[dim + 1], *dims[dim + 2 :])


def sent_to_all(shard, axis):
    copies = jnp.broadcast_to(shard, (lax.axis_size(axis), *shard.shape))
    return lax.all_to_all(copies, axis, split_axis=0, concat_axis=0, tiled=True)


def collect(shard, axis, dim):
    return laid_out(sent_to_all(shard, axis), dim)


def in_one_piece(arrays, axis, dim, along):
    widths = [a.shape[along] for a in arrays]
    both = jnp.concatenate(arrays, axis=along)
    whole = lax.all_gather(both, axis, axis=dim, tiled=True)
    return tuple(jnp.split(whole, [sum(widths[:k]) for k in range(1, len(widths))], axis=along))


def over_copies(shard, axis):
    everything = sent_to_all(shard, axis)
    return jnp.sum(everything, axis=0)


def in_one(arrays, axis):
    ends = [0]
    for a in arrays:
        ends.append(ends[-1] + a.size)
    total = over_copies(jnp.concatenate([a.ravel() for a in arrays]), axis)
    return tuple((total[b:e].reshape(a.shape) for a, b, e in zip(arrays, ends, ends[1:])))


def kernel_block(target, source):
    products = jnp.einsum("id,kjd->kij", target, source, preferred_element_type=jnp.float32)
    target_sq = jnp.sum(jnp.square(target.astype(jnp.float32)), axis=-1)
    source_sq = jnp.sum(jnp.square(source.astype(jnp.float32)), axis=-1)
    distance = target_sq[None, :, None] + source_sq[:, None, :] - 2.0 * products
    return jnp.exp(-kernel_rate * distance).astype(jnp.bfloat16)


def kernel_pair(target, target_sq, source):
    products = jnp.dot(target, source.T, preferred_element_type=jnp.float32)
    source_sq = jnp.sum(jnp.square(source.astype(jnp.float32)), axis=-1)
    distance = target_sq[:, None] + source_sq[None, :] - 2.0 * products
    return jnp.exp(-kernel_rate * distance).astype(jnp.bfloat16)


def slot_table(needed):
    slot_ranks = jnp.cumsum(needed.astype(jnp.int32), axis=1) - 1
    matches = needed[:, :, None] & (
        slot_ranks[:, :, None] == jnp.arange(CAP, dtype=jnp.int32)[None, None, :]
    )
    member_ids = jnp.arange(needed.shape[1], dtype=jnp.int32)
    chosen = jnp.sum(matches.astype(jnp.int32) * member_ids[None, :, None], axis=1)
    return (slot_ranks, chosen)


def body(
    points,
    charges,
    near_leaves,
    leaf_interpolant,
    skel_leaf,
    interp_mid,
    skel_mid,
    mid_partners,
    interp_top,
    skel_top,
):
    group_size = lax.axis_size("sub")
    self_index = lax.axis_index("sub")
    leaf_dev = leaf_interpolant.shape[0]
    leaf_size = leaf_interpolant.shape[1]
    coords = points.shape[1]
    rhs_count = charges.shape[1]
    near_count = near_leaves.shape[1]
    group_first = lax.axis_index("leaf") * group_size
    leaf_base = group_first * leaf_dev
    point_blocks = points.reshape(leaf_dev, leaf_size, coords)
    charge_blocks = charges.reshape(leaf_dev, leaf_size, rhs_count)
    local_ids = near_leaves - leaf_base
    owners = local_ids // leaf_dev
    members = local_ids % leaf_dev
    slots_all = jnp.arange(group_size * leaf_dev, dtype=jnp.int32)
    others = (jnp.arange(group_size, dtype=jnp.int32) != self_index)[:, None]
    wanted = (
        jnp.any(local_ids[:, :, None] == slots_all[None, None, :], axis=(0, 1)).reshape(
            group_size, leaf_dev
        )
        & others
    )
    slot_ranks, chosen = slot_table(wanted)
    listed = collect(near_leaves, "sub", 0).reshape(group_size, -1)
    my_leaves = leaf_base + self_index * leaf_dev + jnp.arange(leaf_dev, dtype=jnp.int32)
    asked_for = jnp.any(listed[:, :, None] == my_leaves[None, None, :], axis=1) & others
    unused, handed = slot_table(asked_for)
    recv_points, recv_charges = (
        lax.all_to_all(point_blocks[handed], "sub", split_axis=0, concat_axis=0, tiled=True),
        lax.all_to_all(charge_blocks[handed], "sub", split_axis=0, concat_axis=0, tiled=True),
    )
    pool_points = jnp.concatenate(
        (point_blocks, recv_points.reshape(-1, leaf_size, coords)), axis=0
    )
    pool_charges = jnp.concatenate(
        (charge_blocks, recv_charges.reshape(-1, leaf_size, rhs_count)), axis=0
    )
    local_flag = owners == self_index
    slot_of = jnp.clip(slot_ranks[owners, members], 0, CAP - 1)
    pool_index = jnp.where(local_flag, members, leaf_dev + owners * CAP + slot_of)

    def near_leaf(leaf_index, totals):
        target = lax.dynamic_index_in_dim(point_blocks, leaf_index, 0, keepdims=False)
        target_sq = jnp.sum(jnp.square(target.astype(jnp.float32)), axis=-1)
        summed = jnp.zeros((leaf_size, rhs_count), jnp.float32)
        for entry in range(near_count):
            source_index = pool_index[leaf_index, entry]
            source = lax.dynamic_index_in_dim(pool_points, source_index, 0, keepdims=False)
            weights = lax.dynamic_index_in_dim(pool_charges, source_index, 0, keepdims=False)
            kernel = kernel_pair(target, target_sq, source)
            summed = summed + jnp.dot(kernel, weights, preferred_element_type=jnp.float32)
        return lax.dynamic_update_slice(totals, summed[None], (leaf_index, 0, 0))

    near_sum = lax.fori_loop(
        0, leaf_dev, near_leaf, jnp.zeros((leaf_dev, leaf_size, rhs_count), jnp.float32)
    )
    leaf_upward = jnp.einsum(
        "tmv,tmz->tvz", leaf_interpolant, charge_blocks, preferred_element_type=jnp.float32
    ).astype(jnp.bfloat16)
    leaf_skel = jnp.take_along_axis(point_blocks, skel_leaf[:, :, None], axis=1)
    mid_up = jnp.einsum(
        "qs,qr->sr",
        interp_mid[0],
        leaf_upward.reshape(-1, rhs_count),
        preferred_element_type=jnp.float32,
    ).astype(jnp.bfloat16)
    mid_points = leaf_skel.reshape(-1, coords)[skel_mid[0]]
    partners = mid_partners[0]
    skel_count = mid_points.shape[0]
    shard_points, shard_weights = in_one_piece((mid_points[None], mid_up[None]), "sub", 0, 2)
    node_ids = group_first + jnp.arange(shard_points.shape[0], dtype=jnp.int32)
    flags = jnp.sum((partners[:, None] == node_ids[None, :]).astype(jnp.float32), axis=0)
    kernel = kernel_block(mid_points, shard_points) * flags.astype(jnp.bfloat16)[:, None, None]
    mid_sum = jnp.einsum("kij,kjr->ir", kernel, shard_weights, preferred_element_type=jnp.float32)
    top_part = jnp.einsum("qs,qr->sr", interp_top[0], mid_up, preferred_element_type=jnp.float32)
    picked = skel_top[0] - self_index * skel_count
    inside = (picked >= 0) & (picked < skel_count)
    top_rows = jnp.where(
        inside[:, None], mid_points[jnp.clip(picked, 0, skel_count - 1)].astype(jnp.float32), 0.0
    )
    top_weight, top_points = in_one((top_part, top_rows), "sub")
    top_weight = top_weight.astype(jnp.bfloat16)
    top_points = top_points.astype(jnp.bfloat16)
    own_group = lax.axis_index("leaf")
    shard_points, shard_weights = in_one_piece((top_points[None], top_weight[None]), "leaf", 0, 2)
    node_ids = jnp.arange(shard_points.shape[0], dtype=jnp.int32)
    flags = (node_ids != own_group).astype(jnp.bfloat16)
    kernel = kernel_block(top_points, shard_points) * flags[:, None, None]
    top_sum = jnp.einsum("kij,kjr->ir", kernel, shard_weights, preferred_element_type=jnp.float32)
    top_sum = top_sum.astype(jnp.bfloat16)
    mid_total = (
        mid_sum + jnp.dot(interp_top[0], top_sum, preferred_element_type=jnp.float32)
    ).astype(jnp.bfloat16)
    leaf_downward = (
        jnp.dot(interp_mid[0], mid_total, preferred_element_type=jnp.float32)
        .astype(jnp.bfloat16)
        .reshape(leaf_dev, -1, rhs_count)
    )
    distant_sum = jnp.einsum(
        "xiv,xvq->xiq", leaf_interpolant, leaf_downward, preferred_element_type=jnp.float32
    )
    return (near_sum + distant_sum).reshape(-1, rhs_count)


def solution(mesh):
    placed = (
        P(("leaf", "sub"), None),
        P(("leaf", "sub"), None),
        P(("leaf", "sub"), None),
        P(("leaf", "sub"), None, None),
        P(("leaf", "sub"), None),
        P(("leaf", "sub"), None, None),
        P(("leaf", "sub"), None),
        P(("leaf", "sub"), None),
        P("leaf", "sub", None),
        P("leaf", None),
    )
    return jax.shard_map(
        body, mesh=mesh, in_specs=placed, out_specs=P(("leaf", "sub"), None), check_vma=False
    )
```

profile of v0, /device:TPU:2, one launch (start us, length us, event | category | flops | bytes accessed | tf_op | source)
XLA Modules:
  0.0 680.5 jit_solution(14890606376546862535)
XLA Ops:
  8.0 8.1 %all-to-all-start = ((s32[16,8,12]{2,1,0:T(8,128)}), s32[16,8,12]{2,1,0:T(8,128)}, u32[]{:S(2)}, u32[]{:S(2)}) async-start(s32[16,8,12]{2,1,0:T(8,128)} %broadcast_in_dim.130), calls=%async_computation | async-start | bytes 131072 | tf_op jit(solution)/shard_map/all_to_all | solution.py:20
  25.0 20.5 %gather_fusion.5 = bf16[2048,128]{1,0:T(8,128)(2,1)} fusion(bf16[8,512,128]{2,1,0:T(8,128)(2,1)S(1)} %bitcast.375, s32[2048]{0:T(1024)S(1)} %bitcast.374), kind=kCustom, calls=%fused_computation.5 | custom fusion | bytes 1064960 | tf_op jit(solution)/shard_map/jit(take_along_axis)/gather | solution.py:143
  56.8 4.2 gather_fusion.2
  61.0 4.8 copy.80
  65.8 7.2 %all-to-all-start.2 = ((bf16[16,2,512,64]{2,3,1,0:T(8,128)(2,1)}), bf16[16,2,512,64]{2,3,1,0:T(8,128)(2,1)}, u32[]{:S(2)}, u32[]{:S(2)}) async-start(bf16[16,2,512,64]{2,3,1,0:T(8,128)(2,1)} %bitcast.383), calls=%async_computation.2 | async-start | bytes 4194304 | tf_op jit(solution)/shard_map/all_to_all | solution.py:113
  75.0 28.5 %all-to-all-done.2 = bf16[16,2,512,64]{2,3,1,0:T(8,128)(2,1)} async-done(((bf16[16,2,512,64]{2,3,1,0:T(8,128)(2,1)}), bf16[16,2,512,64]{2,3,1,0:T(8,128)(2,1)}, u32[]{:S(2)}, u32[]{:S(2)}) %all-to-all-start.2) | async-done | bytes 2097184 | tf_op jit(solution)/shard_map/all_to_all | solution.py:113
  103.4 4.1 broadcast_in_dim.138
  107.5 4.6 all-to-all-start.3
  113.1 3.1 gather_fusion.1
  116.2 41.2 %all-to-all-done.3 = f32[16,1,49152]{2,1,0:T(1,128)} async-done(((f32[16,1,49152]{2,1,0:T(1,128)}), f32[16,1,49152]{2,1,0:T(1,128)}, u32[]{:S(2)}, u32[]{:S(2)}) %all-to-all-start.3) | async-done | bytes 3145760 | tf_op jit(solution)/shard_map/all_to_all | solution.py:20
  157.4 4.9 all-to-all-start.1
  165.7 4.8 copy.81
  170.6 5.8 pad_maximum_fusion.1
  176.4 38.1 %all-gather.2.cloned.1.call-done = bf16[16,256,192]{1,2,0:T(8,128)(2,1)} async-done(((bf16[1,256,192]{1,2,0:T(8,128)(2,1)}), bf16[16,256,192]{1,2,0:T(8,128)(2,1)}) %all-gather.2.cloned.1.call-update) | async-done | bytes 1572880 | tf_op jit(solution)/shard_map/all_gather | solution.py:30
  219.0 3.9 reduce_sum.239
  224.8 13.5 %all_gather.7 = bf16[8,256,192]{1,2,0:T(8,128)(2,1)S(1)} all-gather(bf16[1,256,192]{1,2,0:T(8,128)(2,1)S(1)} %copy.90), channel_id=1, replica_groups=mesh['leaf'=8,'sub'=16] {'leaf'}, dimensions={0}, use_global_device_ids=true | all-gather | bytes 884736 | tf_op jit(solution)/shard_map/all_gather | solution.py:30
  245.5 2.7 fusion.296
  248.2 3.6 fusion.291
  253.7 5.0 pad_maximum_fusion
  258.7 411.9 %while.13 = (s32[]{:T(128)}, f32[8,512,64]{1,2,0:T(8,128)}, bf16[8,512,128]{2,1,0:T(8,128)(2,1)S(1)}, s32[8,12]{1,0:T(8,128)S(1)}, bf16[40,512,128]{2,1,0:T(8,12...) while((s32[]{:T(128)}, f32[8,512,64]{1,2,0:T(8,128)}, ...), condition=%wide.region_19.20_spmd, body=%wide.region_5.19_spmd.sunk | while | flops 1226597888 | bytes 9532565 | solution.py:137
  281.5 2.4 multiply_reduce_fusion.18
  332.9 2.4 multiply_reduce_fusion.18
  384.4 2.4 multiply_reduce_fusion.18
  435.9 2.4 multiply_reduce_fusion.18
  (206 shorter events, 271.8 us)
Async XLA Ops:
  6.5 16.7 %copy-start = (bf16[8,512,256]{2,1,0:T(8,128)(2,1)S(1)}, bf16[8,512,256]{2,1,0:T(8,128)(2,1)}, u32[]{:S(2)}) copy-start(bf16[8,512,256]{2,1,0:T(8,128)(2,1)} %param.15) | copy-start | bytes 6291460
  6.5 18.5 %copy-start.1 = (bf16[4096,128]{1,0:T(8,128)(2,1)S(1)}, bf16[4096,128]{1,0:T(8,128)(2,1)}, u32[]{:S(2)}) copy-start(bf16[4096,128]{1,0:T(8,128)(2,1)} %param.12) | copy-start | bytes 3145732
  8.0 45.6 %all-to-all-start = ((s32[16,8,12]{2,1,0:T(8,128)}), s32[16,8,12]{2,1,0:T(8,128)}, u32[]{:S(2)}, u32[]{:S(2)}) async-start(s32[16,8,12]{2,1,0:T(8,128)} %broadcast_in_dim.130), calls=%async_computation | async-start | bytes 131072 | tf_op jit(solution)/shard_map/all_to_all | solution.py:20
  18.8 1.4 copy-start.6
  23.2 26.6 %copy-start.3 = (bf16[1,256,256]{2,1,0:T(8,128)(2,1)S(1)}, bf16[1,256,256]{2,1,0:T(8,128)(2,1)}, u32[]{:S(2)}) copy-start(bf16[1,256,256]{2,1,0:T(8,128)(2,1)} %param.20) | copy-start | bytes 393220
  49.3 0.6 copy-start.4
  61.0 12.0 %copy-start.9 = (s32[1,256]{1,0:T(1,128)S(1)}, s32[1,256]{1,0:T(1,128)}, u32[]{:S(2)}) copy-start(s32[1,256]{1,0:T(1,128)} %param.21) | copy-start | bytes 3076
  65.8 37.6 %all-to-all-start.2 = ((bf16[16,2,512,64]{2,3,1,0:T(8,128)(2,1)}), bf16[16,2,512,64]{2,3,1,0:T(8,128)(2,1)}, u32[]{:S(2)}, u32[]{:S(2)}) async-start(bf16[16,2,512,64]{2,3,1,0:T(8,128)(2,1)} %bitcast.383), calls=%async_computation.2 | async-start | bytes 4194304 | tf_op jit(solution)/shard_map/all_to_all | solution.py:113
  107.5 4.7 copy-start.5
  107.5 49.9 %all-to-all-start.3 = ((f32[16,1,49152]{2,1,0:T(1,128)}), f32[16,1,49152]{2,1,0:T(1,128)}, u32[]{:S(2)}, u32[]{:S(2)}) async-start(f32[16,1,49152]{2,1,0:T(1,128)} %broadcast_in_dim.138), calls=%async_computation.3 | async-start | bytes 6291456 | tf_op jit(solution)/shard_map/all_to_all | solution.py:20
  112.1 102.4 %all-gather.2.cloned.1.call-start = ((), (), s32[]{:S(2)}) async-start(), calls=%async_computation.4 | async-start | bytes 1671168 | tf_op jit(solution)/shard_map/all_gather | solution.py:30
  116.2 46.7 %copy-start.11 = (s32[1,4]{1,0:T(1,128)S(1)}, s32[1,4]{1,0:T(1,128)}, u32[]{:S(2)}) copy-start(s32[1,4]{1,0:T(1,128)} %param.19) | copy-start | bytes 52
  116.2 48.0 %copy-start.8 = (s32[16,8]{1,0:T(8,128)S(1)}, s32[16,8]{1,0:T(8,128)}, u32[]{:S(2)}) copy-start(s32[16,8]{1,0:T(8,128)} %get-tuple-element.156) | copy-start | bytes 1540
  157.4 8.4 %copy-start.7 = (s32[8,12]{1,0:T(8,128)S(1)}, s32[8,12]{1,0:T(8,128)}, u32[]{:S(2)}) copy-start(s32[8,12]{1,0:T(8,128)} %copy-done.6) | copy-start | bytes 1156
  157.4 96.3 %all-to-all-start.1 = ((bf16[16,2,512,128]{3,2,1,0:T(8,128)(2,1)}), bf16[16,2,512,128]{3,2,1,0:T(8,128)(2,1)}, u32[]{:S(2)}, u32[]{:S(2)}) async-start(bf16[16,2,512,128]{3,2,1,0:T(8,128)(2,1)} %bitcast.382), calls=%async_computation.1 | async-start | bytes 8388608 | tf_op jit(solution)/shard_map/all_to_all | solution.py:112
  223.0 25.2 %copy-start.10 = (f32[256]{0:T(256)S(1)}, f32[256]{0:T(256)}, u32[]{:S(2)}) copy-start(f32[256]{0:T(256)} %multiply_reduce_fusion.16) | copy-start | bytes 3076
  238.3 0.9 copy-start.2
Sparse Core Ops, SparseCore 0:
  115.1 99.3 all-gather.1
where the time goes:
time: 688 us; the launch traced here: 680 us
  matrix products  224 us (33%)
  loops' own time  177 us (26%)
  waiting for transfers between devices  108 us (16%)
  local copies, waits for them, and re-layouts  70.2 us (10%)
  other arithmetic  49.9 us (7%)
  starting transfers between devices  24.8 us (4%)
  between operations  13.7 us (2%)
  blocking collectives  13.5 us (2%)
    dot_general x96, matrix products, near_leaf(): jnp.dot(kernel, weights, preferred_element_type=jnp.float32)  210 us
    another operation x1, loops' own time, body(): lax.fori_loop(0, leaf_dev, near_leaf, jnp.zeros((leaf_dev, leaf_size, rhs...  177 us
    all_to_all x2, waiting for transfers between devices, sent_to_all(): return lax.all_to_all(copies, axis, split_axis=0, concat_axis=0, tiled=True)  41.2 us
    all_gather x1, waiting for transfers between devices, in_one_piece(): whole = lax.all_gather(both, axis, axis=dim, tiled=True)  38.1 us
    all_to_all x1, waiting for transfers between devices, body(): lax.all_to_all(charge_blocks[handed], 'sub', split_axis=0, concat_axis=0,...  28.5 us
    gather x1, local copies, waits for them, and re-layouts, body(): leaf_skel = jnp.take_along_axis(point_blocks, skel_leaf[:, :, None], axis=1)  20.5 us
    reduce_sum x8, other arithmetic, kernel_pair(): source_sq = jnp.sum(jnp.square(source.astype(jnp.float32)), axis=-1)  19.4 us
  transfers between devices with their start and end apart: 5, of which 3 were waited for; matrix products, arithmetic and copies ran while one was open for 12% of the time, Pallas kernels for 0%

commit v1 on v0

v1 whole, which is shorter than its diff:
```python
import jax
import jax.numpy as jnp
from jax import lax
from jax.experimental import pallas as pl
from jax.experimental.pallas import tpu as pltpu
from jax.sharding import PartitionSpec as P

F32, BF16, I32 = jnp.float32, jnp.bfloat16, jnp.int32
MESH = pl.DeviceIdType.MESH

RATE = 0.5 * 1.4426950408889634

N_SUB, N_LEAF = 16, 8
LEAVES, LEAF, DIM, RHS, SKEL, NEAR = 8, 512, 128, 64, 256, 12
PACKED = RHS * LEAF // DIM
SLOT = LEAF + PACKED
MID = SKEL + RHS * SKEL // DIM
HALF = MID // 2

GROUPS = ((6, 12), (4, 14), (9, 3), (1, 11), (10,), (5, 15), (7, 13), (2, 8))
WINDOW = 3


def dot(a, b):
    return jnp.dot(a, b, preferred_element_type=F32)


def dot_nt(a, b):
    return lax.dot_general(a, b, (((1,), (1,)), ((), ())), preferred_element_type=F32)


def pieces(x):
    hi = x.astype(BF16).astype(F32)
    mid = (x - hi).astype(BF16).astype(F32)
    return hi, mid, x - hi - mid


def source_side(rows):
    wide = rows.astype(F32)
    square = wide * wide
    high = square.astype(BF16)
    low = (square - high.astype(F32)).astype(BF16)
    half = jnp.full((2 * DIM, DIM), 0.5, BF16)
    hi, mid, lo = pieces(dot(jnp.concatenate((high, low), axis=1), half))
    lane = lax.broadcasted_iota(I32, hi.shape, 1)
    tail = jnp.where(lane < 6, 1.0, 0.0)
    return jnp.where(lane == 0, hi, jnp.where(lane == 1, mid, jnp.where(lane == 2, lo, tail))).astype(BF16)


def target_side(columns):
    wide = columns.astype(F32)
    half = 0.5 * jnp.sum(wide * wide, axis=0, keepdims=True)
    hi, mid, lo = pieces(half)
    row = lax.broadcasted_iota(I32, (16, columns.shape[1]), 0)
    head = jnp.where(row < 3, -1.0, 0.0)
    made = jnp.where(row == 3, -hi, jnp.where(row == 4, -mid, jnp.where(row == 5, -lo, head)))
    return jnp.concatenate((columns, made.astype(BF16), jnp.zeros((DIM - 16, columns.shape[1]), BF16)), axis=0)


def weighted(sources, weights, targets):
    kernel = jnp.exp2(dot(sources, targets) * RATE).astype(BF16)
    return dot(weights, kernel)


def unpacked(block):
    rows = block.shape[0] // RHS
    return jnp.concatenate([block[c * RHS : (c + 1) * RHS] for c in range(rows)], axis=1)


def packed(wide):
    return jnp.concatenate([wide[:, c : c + DIM] for c in range(0, wide.shape[1], DIM)], axis=0)


def exchange_kernel(
    points, charges, near, near_smem, interp_hbm, skel_leaf, mid_hbm, skel_mid, partners, top, skel_top,
    recv, total, targets,
    interp, interp_mid, lists, list_in, charge_pack, send, own_side, skel_cols,
    mid_a, mid_b, scatter, scatter_in, gathered, crossed,
    local_sem, list_s, list_r, near_s, near_r, ma_s, ma_r, mb_s, mb_r, sc_s, sc_r, ga_s, ga_r, cr_s, cr_r,
):
    me, group = lax.axis_index("sub"), lax.axis_index("leaf")
    z, y = me // 4, me % 4
    base = (group * N_SUB + me) * LEAVES

    def peer(k):
        return ((z + k // 4) % 4) * 4 + (y + k % 4) % 4

    def remote(src, dst, s, r, to):
        return pltpu.make_async_remote_copy(
            src_ref=src, dst_ref=dst, send_sem=s, recv_sem=r, device_id=to, device_id_type=MESH
        )

    def in_sub(src, dst, s, r, k):
        return remote(src, dst, s, r, (group, peer(k)))

    load_interp = pltpu.make_async_copy(interp_hbm, interp, local_sem.at[0])
    load_mid = pltpu.make_async_copy(mid_hbm, interp_mid, local_sem.at[1])
    load_interp.start()
    load_mid.start()

    barrier = pltpu.get_barrier_semaphore()
    for k in range(1, N_SUB):
        pl.semaphore_signal(barrier, inc=1, device_id=(group, peer(k)), device_id_type=MESH)
    for j in range(1, N_LEAF):
        pl.semaphore_signal(barrier, inc=1, device_id=((group + j) % N_LEAF, me), device_id_type=MESH)
    lists[...] = jnp.full(lists.shape, -1, I32)
    lists[:, :NEAR] = near[...]
    pl.semaphore_wait(barrier, N_SUB + N_LEAF - 2)

    list_copies = [None] + [
        in_sub(lists, list_in.at[k], list_s.at[k], list_r.at[k], k) for k in range(1, N_SUB)
    ]
    order = [k for ks in GROUPS for k in ks]
    for k in order:
        list_copies[k].start()

    @pl.loop(0, LEAVES)
    def _(l):
        charge_pack[l] = packed(jnp.transpose(charges[l]))

    steps = [(ks, s) for ks in GROUPS for s in range(2)]
    near_copies = []
    chosen = {}

    def advance():
        t = len(near_copies)
        if t >= len(steps):
            return
        if t >= WINDOW:
            for c in near_copies[t - WINDOW]:
                c.wait_send()
        ks, s = steps[t]
        started = []
        for k in ks:
            if s == 0:
                back = (-(k // 4)) % 4 * 4 + (-k) % 4
                list_copies[back].wait_recv()
                here = list_in[back] - base
                inside = (here >= 0) & (here < LEAVES)
                chosen[k] = (
                    jnp.min(jnp.where(inside, here, LEAVES - 1)),
                    jnp.max(jnp.where(inside, here, 0)),
                )
            leaf = chosen[k][s]
            send[k, s, :LEAF, :] = points[leaf]
            send[k, s, LEAF:, :] = charge_pack[leaf]
            c = in_sub(send.at[k, s], recv.at[k, s], near_s.at[k, s], near_r.at[k, s], k)
            c.start()
            started.append(c)
        near_copies.append(started)

    for _ in range(WINDOW):
        advance()

    load_interp.wait()
    load_mid.wait()
    up = jnp.zeros((RHS, SKEL), F32)
    rows_in_leaf = lax.broadcasted_iota(I32, (LEAF, SKEL), 0)

    def upward(l, up):
        columns = jnp.transpose(points[l])
        targets[l] = target_side(columns)
        picks = jnp.where(rows_in_leaf == skel_leaf[pl.ds(l, 1), :], 1.0, 0.0).astype(BF16)
        skel_cols[l] = dot(columns, picks).astype(BF16)
        leaf_up = dot(unpacked(charge_pack[l]), interp[l]).astype(BF16)
        return up + dot(leaf_up, interp_mid[pl.ds(pl.multiple_of(l * SKEL, SKEL), SKEL), :])

    up = lax.fori_loop(0, LEAVES, upward, up)
    mid_up = up.astype(BF16)

    def pick_mid(l, cols):
        row = lax.broadcasted_iota(I32, (SKEL, SKEL), 0) + l * SKEL
        picks = jnp.where(row == skel_mid[...], 1.0, 0.0).astype(BF16)
        return cols + dot(skel_cols[l], picks)

    mid_cols = lax.fori_loop(0, LEAVES, pick_mid, jnp.zeros((DIM, SKEL), F32))
    mid_rows = jnp.transpose(mid_cols).astype(BF16)
    own_mid = jnp.concatenate((mid_rows, packed(mid_up)), axis=0)
    mid_a[0, 0] = own_mid[:HALF]
    mid_b[0, 0] = own_mid[HALF:]
    first = []
    for d in (1, 3, 2):
        first.append((in_sub(mid_a.at[0, 0], mid_a.at[0, d], ma_s.at[0, d], ma_r.at[0, d], d),
                      in_sub(mid_b.at[0, 0], mid_b.at[0, d], mb_s.at[0, d], mb_r.at[0, d], 4 * d)))
        for c in first[-1]:
            c.start()

    row = lax.broadcasted_iota(I32, (SKEL, SKEL), 0) + me * SKEL
    picks = jnp.where(row == skel_top[...], 1.0, 0.0).astype(BF16)
    top_part = jnp.concatenate((dot(mid_up, top[...]), jnp.zeros((DIM - RHS, SKEL), F32)), axis=0)
    scatter[:, :DIM] = jnp.transpose(top_part)
    scatter[:, DIM:] = jnp.transpose(dot(mid_cols.astype(BF16), picks))
    piece = SKEL // N_SUB

    def rows_of(index):
        return pl.ds(pl.multiple_of(index * piece, piece), piece)

    scatter_copies = []
    for k in order:
        c = in_sub(scatter.at[rows_of(peer(k))], scatter_in.at[k], sc_s.at[k], sc_r.at[k], k)
        c.start()
        scatter_copies.append(c)
    advance()

    @pl.loop(0, LEAVES)
    def _(l):
        own_side[l] = source_side(points[l])

    def own_pairs(l):
        result = jnp.zeros((RHS, LEAF), F32)
        for part in range(0, LEAVES, 4):
            rows, weights = [], []
            for m in range(part, part + 4):
                named = near_smem[l, 0] == base + m
                for e in range(1, NEAR):
                    named = named | (near_smem[l, e] == base + m)
                flag = jnp.where(named, 1.0, 0.0)
                rows.append(jnp.concatenate((points[m], own_side[m]), axis=1))
                weights.append((unpacked(charge_pack[m]).astype(F32) * flag).astype(BF16))
            result += weighted(jnp.concatenate(rows, axis=0), jnp.concatenate(weights, axis=1), targets[l])
        total[l] = result

    def own_chunk(begin, end):
        pl.loop(begin, end)(own_pairs)

    own_chunk(0, 2)
    advance()

    for pair in first:
        for c in pair:
            c.wait_recv()
    second = []
    for d in (1, 3, 2):
        second.append((in_sub(mid_a.at[0], mid_a.at[d], ma_s.at[1, d], ma_r.at[1, d], 4 * d),
                       in_sub(mid_b.at[0], mid_b.at[d], mb_s.at[1, d], mb_r.at[1, d], d)))
        for c in second[-1]:
            c.start()
    advance()

    for c in scatter_copies:
        c.wait_recv()
    summed = scatter[rows_of(me), :]
    for k in range(1, N_SUB):
        summed = summed + scatter_in[k]
    gathered[rows_of(me), :] = summed.astype(BF16)
    gather_copies = []
    for k in order:
        c = in_sub(gathered.at[rows_of(me)], gathered.at[rows_of(me)], ga_s.at[k], ga_r.at[k], k)
        c.start()
        gather_copies.append(c)

    own_chunk(2, 4)
    advance()
    own_chunk(4, 6)
    advance()

    for c in gather_copies:
        c.wait_recv()
    cross_copies = []
    for j in (1, 7, 2, 6, 3, 5, 4):
        c = remote(gathered, crossed.at[j - 1], cr_s.at[j - 1], cr_r.at[j - 1], ((group + j) % N_LEAF, me))
        c.start()
        cross_copies.append(c)
    own_chunk(6, 8)
    advance()
    advance()

    for pair in second:
        for c in pair:
            c.wait_recv()
    mid_targets = target_side(mid_cols.astype(BF16))
    rows, weights = [], []
    for p in range(4):
        node = partners[0, p] - group * N_SUB
        dz, dy = (z + 4 - node // 4) % 4, (y + 4 - node % 4) % 4
        block = jnp.concatenate((mid_a[dz, dy], mid_b[dy, dz]), axis=0)
        rows.append(jnp.concatenate((block[:SKEL], source_side(block[:SKEL])), axis=1))
        weights.append(unpacked(block[SKEL:]))
    mid_sum = weighted(jnp.concatenate(rows, axis=0), jnp.concatenate(weights, axis=1), mid_targets)
    advance()

    for c in cross_copies:
        c.wait_recv()
    top_targets = target_side(jnp.transpose(gathered[:, DIM:].astype(F32)).astype(BF16))

    def top_from(j, acc):
        rows = crossed[j, :, DIM:]
        weights = jnp.transpose(crossed[j, :, :DIM].astype(F32)).astype(BF16)[:RHS]
        return acc + weighted(jnp.concatenate((rows, source_side(rows)), axis=1), weights, top_targets)

    top_sum = lax.fori_loop(0, N_LEAF - 1, top_from, jnp.zeros((RHS, SKEL), F32)).astype(BF16)
    mid_total = (mid_sum + dot_nt(top_sum, top[...])).astype(BF16)
    advance()

    @pl.loop(0, LEAVES)
    def _(l):
        down = dot_nt(mid_total, interp_mid[pl.ds(pl.multiple_of(l * SKEL, SKEL), SKEL), :]).astype(BF16)
        total[l] += dot_nt(down, interp[l])

    while len(near_copies) < len(steps):
        advance()
    for t, copies in enumerate(near_copies):
        for c in copies:
            if t >= len(steps) - WINDOW:
                c.wait_send()
            c.wait_recv()
    for c in list_copies[1:] + scatter_copies + gather_copies + cross_copies:
        c.wait_send()
    for pair in first + second:
        for c in pair:
            c.wait_send()


def near_kernel(near, recv, targets, total, out, side, listed, count, lowest, used):
    me, group = lax.axis_index("sub"), lax.axis_index("leaf")
    z, y = me // 4, me % 4
    base = group * N_SUB * LEAVES

    for i in range(N_SUB):
        lowest[i] = LEAVES
    for i in range(2 * N_SUB):
        used[i] = 0

    @pl.loop(0, LEAVES)
    def _(l):
        for e in range(1, NEAR):
            named = near[l, e] - base
            owner, leaf = named // LEAVES, named % LEAVES
            lowest[owner] = jnp.minimum(lowest[owner], leaf)

    @pl.loop(0, LEAVES)
    def _(l):
        held = jnp.int32(0)
        for e in range(1, NEAR):
            named = near[l, e] - base
            owner, leaf = named // LEAVES, named % LEAVES
            shift = ((z + 4 - owner // 4) % 4) * 4 + (y + 4 - owner % 4) % 4
            slot = 2 * shift + jnp.where(leaf == lowest[owner], 0, 1)
            listed[l, held] = slot
            there = jnp.where(owner == me, 0, 1)
            used[slot] = jnp.maximum(used[slot], there)
            held = held + there
        count[l] = held

    @pl.loop(2, 2 * N_SUB)
    def _(i):
        @pl.when(used[i] > 0)
        def _():
            side[i] = source_side(recv[i, :LEAF, :])

    @pl.loop(0, LEAVES)
    def _(l):
        held = count[l]

        def four(n, acc):
            rows, weights = [], []
            for u in range(4):
                e = n * 4 + u
                real = e < held
                slot = listed[l, jnp.where(real, e, 0)]
                rows.append(jnp.concatenate((recv[slot, :LEAF, :], side[slot]), axis=1))
                flag = jnp.where(real, 1.0, 0.0)
                weights.append((unpacked(recv[slot, LEAF:, :]).astype(F32) * flag).astype(BF16))
            return acc + weighted(jnp.concatenate(rows, axis=0), jnp.concatenate(weights, axis=1), targets[l])

        acc = lax.fori_loop(0, (held + 3) // 4, four, total[l])
        out[l] = jnp.transpose(acc)


def body(
    points, charges, near_leaves, leaf_interpolant, skel_leaf,
    interp_mid, skel_mid, mid_partners, interp_top, skel_top,
):
    vmem, smem, hbm = (pl.BlockSpec(memory_space=m) for m in (pltpu.VMEM, pltpu.SMEM, pl.ANY))
    dma = pltpu.SemaphoreType.DMA
    recv, total, targets = pl.pallas_call(
        exchange_kernel,
        out_shape=(
            jax.ShapeDtypeStruct((N_SUB, 2, SLOT, DIM), BF16),
            jax.ShapeDtypeStruct((LEAVES, RHS, LEAF), F32),
            jax.ShapeDtypeStruct((LEAVES, 2 * DIM, LEAF), BF16),
        ),
        in_specs=[vmem, vmem, vmem, smem, hbm, vmem, hbm, vmem, smem, vmem, vmem],
        out_specs=(hbm, vmem, vmem),
        scratch_shapes=[
            pltpu.VMEM((LEAVES, LEAF, SKEL), BF16),
            pltpu.VMEM((LEAVES * SKEL, SKEL), BF16),
            pltpu.VMEM((LEAVES, DIM), I32),
            pltpu.VMEM((N_SUB, LEAVES, DIM), I32),
            pltpu.VMEM((LEAVES, PACKED, DIM), BF16),
            pltpu.VMEM((N_SUB, 2, SLOT, DIM), BF16),
            pltpu.VMEM((LEAVES, LEAF, DIM), BF16),
            pltpu.VMEM((LEAVES, DIM, SKEL), BF16),
            pltpu.VMEM((4, 4, HALF, DIM), BF16),
            pltpu.VMEM((4, 4, HALF, DIM), BF16),
            pltpu.VMEM((SKEL, 2 * DIM), F32),
            pltpu.VMEM((N_SUB, SKEL // N_SUB, 2 * DIM), F32),
            pltpu.VMEM((SKEL, 2 * DIM), BF16),
            pltpu.VMEM((N_LEAF - 1, SKEL, 2 * DIM), BF16),
            dma((2,)),
            dma((N_SUB,)), dma((N_SUB,)),
            dma((N_SUB, 2)), dma((N_SUB, 2)),
            dma((2, 4)), dma((2, 4)), dma((2, 4)), dma((2, 4)),
            dma((N_SUB,)), dma((N_SUB,)),
            dma((N_SUB,)), dma((N_SUB,)),
            dma((N_LEAF - 1,)), dma((N_LEAF - 1,)),
        ],
        compiler_params=pltpu.CompilerParams(
            collective_id=0, has_side_effects=True, vmem_limit_bytes=56 << 20
        ),
    )(
        points.reshape(LEAVES, LEAF, DIM), charges.reshape(LEAVES, LEAF, RHS), near_leaves, near_leaves,
        leaf_interpolant, skel_leaf, interp_mid[0], skel_mid, mid_partners, interp_top[0], skel_top,
    )
    out = pl.pallas_call(
        near_kernel,
        out_shape=jax.ShapeDtypeStruct((LEAVES, LEAF, RHS), F32),
        in_specs=[smem, vmem, vmem, vmem],
        out_specs=vmem,
        scratch_shapes=[
            pltpu.VMEM((2 * N_SUB, LEAF, DIM), BF16),
            pltpu.SMEM((LEAVES, 16), I32),
            pltpu.SMEM((LEAVES,), I32),
            pltpu.SMEM((N_SUB,), I32),
            pltpu.SMEM((2 * N_SUB,), I32),
        ],
        compiler_params=pltpu.CompilerParams(vmem_limit_bytes=56 << 20),
    )(near_leaves, recv.reshape(2 * N_SUB, SLOT, DIM), targets, total)
    return out.reshape(LEAVES * LEAF, RHS)


def solution(mesh):
    placed = (
        P(("leaf", "sub"), None),
        P(("leaf", "sub"), None),
        P(("leaf", "sub"), None),
        P(("leaf", "sub"), None, None),
        P(("leaf", "sub"), None),
        P(("leaf", "sub"), None, None),
        P(("leaf", "sub"), None),
        P(("leaf", "sub"), None),
        P("leaf", "sub", None),
        P("leaf", None),
    )
    return jax.shard_map(
        body, mesh=mesh, in_specs=placed, out_specs=P(("leaf", "sub"), None), check_vma=False
    )
```

time: 688 us -> 158 us (0.23)
  the two profiles are of different devices: /device:TPU:2 before, /device:TPU:12 now
where the time goes in v1:
time: 158 us
  Pallas kernels  152 us (96%)
  local copies, waits for them, and re-layouts  5.5 us (3%)
    pallas_call x1, Pallas kernels, body(): pl.pallas_call(exchange_kernel, out_shape=(jax.ShapeDtypeStruct((N_SUB, 2...  118 us
    pallas_call x1, Pallas kernels, body(): pl.pallas_call(near_kernel, out_shape=jax.ShapeDtypeStruct((LEAVES, LEAF,...  34.1 us

profile of v1, /device:TPU:12, one launch (start us, length us, event | category | flops | bytes accessed | tf_op | source)
XLA Modules:
  0.0 157.9 jit_solution(16829469257629470855)
XLA Ops:
  0.0 2.4 %copy.11 = bf16[4096,64]{1,0:T(8,128)(2,1)} copy(bf16[4096,64]{0,1:T(8,128)(2,1)} %param.11) | data formatting | bytes 1048576 | tf_op args[1]
  2.4 118.2 %shard_map.100 = (bf16[16,2,768,128]{3,2,1,0:T(8,128)(2,1)}, f32[8,64,512]{2,1,0:T(8,128)}, bf16[8,256,512]{2,1,0:T(8,128)(2,1)}) custom-call(bf16[8,512,128]{2,1,0:T(8,128)(2,1)} %bitcast.9, bf16[8,512,64]{2,1,0:T(8,128)(2,1)} %bitcast.8, s32[8,12]{1,0:T(8,128)} %near.3, s32[8,12]{1,0:T(8,128)} %near.3, bf16[8,512,256]{2,1,0:T(8,128)(2,1)} %interp_hbm.1, ...), custom_call_target="tpu_custom_call" | custom-call | tf_op jit(solution)/shard_map/pallas_call | solution.py:376
  120.6 34.1 %shard_map.101 = f32[8,512,64]{2,1,0:T(8,128)} custom-call(s32[8,12]{1,0:T(8,128)} %near.3, bf16[32,768,128]{2,1,0:T(8,128)(2,1)} %bitcast.7, bf16[8,256,512]{2,1,0:T(8,128)(2,1)} %get-tuple-element.9.targets, f32[8,64,512]{2,1,0:T(8,128)} %get-tuple-element.10.total), custom_call_target="tpu_custom_call" | custom-call | tf_op jit(solution)/shard_map/pallas_call | solution.py:415
  154.8 3.1 %copy.12 = f32[4096,64]{0,1:T(8,128)} copy(f32[4096,64]{1,0:T(8,128)} %bitcast.6) | data formatting | bytes 2097152 | tf_op jit(solution)/shard_map/reshape | solution.py:429

commit v2 on v1

--- a/solution.py
+++ b/solution.py
@@ -18,7 +18,10 @@
 HALF = MID // 2
 
 GROUPS = ((6, 12), (4, 14), (9, 3), (1, 11), (10,), (5, 15), (7, 13), (2, 8))
-WINDOW = 3
+WINDOW = 5
+ORDER = [k for ks in GROUPS for k in ks]
+EARLY, MIDDLE = 8, 11
+STAGE = 64
 
 
 def dot(a, b):
@@ -71,11 +74,62 @@
     return jnp.concatenate([wide[:, c : c + DIM] for c in range(0, wide.shape[1], DIM)], axis=0)
 
 
+def sorted_lists(lists, first_leaf, z, y):
+    shape = (128, 128)
+    sub, lane = lax.broadcasted_iota(I32, shape, 0), lax.broadcasted_iota(I32, shape, 1)
+
+    def down(row):
+        return jnp.transpose(jnp.broadcast_to(row.astype(F32), shape)).astype(I32)
+
+    tall = jnp.concatenate([jnp.broadcast_to(lists[l : l + 1, :], (16, 128)) for l in range(LEAVES)], axis=0)
+    mine = jnp.where((sub % 16 == lane) & (sub % 16 < NEAR), tall - first_leaf, 0)
+    column = jnp.broadcast_to(jnp.sum(mine.astype(F32), axis=1, keepdims=True), shape)
+    va, vb = column.astype(I32), jnp.transpose(column).astype(I32)
+    before = (sub % 16 < NEAR) & (va // LEAVES == vb // LEAVES) & (va < vb)
+    slot = jnp.max(jnp.where(before, 1.0, 0.0), axis=0, keepdims=True).astype(I32)
+    owner, place = vb[:1] // LEAVES, lane[:1] % 16
+    shift = (z + 4 - owner // 4) % 4 * 4 + (y + 4 - owner % 4) % 4
+    turn = jnp.zeros_like(shift)
+    for at, k in enumerate(ORDER):
+        turn = jnp.where(shift == k, at, turn)
+    stage = jnp.where(turn < EARLY, 0, jnp.where(turn < MIDDLE, 1, 2))
+    stage = jnp.where(place < NEAR, jnp.where(shift == 0, 3, stage), 4)
+    key, code = stage * 16 + place, stage * STAGE + 2 * turn + slot
+    same = sub // 16 == lane // 16
+    rank = jnp.sum(jnp.where(same & (down(key) < key), 1.0, 0.0), axis=0, keepdims=True).astype(I32)
+    chosen = jnp.where(same & (down(rank) == lane % 16), down(code), 0)
+    return jnp.sum(chosen.astype(F32), axis=0, keepdims=True).astype(I32)
+
+
+def progress(codes, l):
+    first = both = remote = jnp.int32(0)
+    for e in range(NEAR):
+        code = codes[0, l * 16 + e]
+        first += jnp.where(code < STAGE, 1, 0)
+        both += jnp.where(code < 2 * STAGE, 1, 0)
+        remote += jnp.where(code < 3 * STAGE, 1, 0)
+    first = jnp.minimum(first, 4)
+    return first, first + jnp.minimum(both - first, 4), remote
+
+
+def listed_pairs(codes, l, start, limit, held, side, target):
+    rows, weights = [], []
+    spare = jnp.where(codes[0, l * 16 + start] < limit, codes[0, l * 16 + start], 0)
+    for u in range(4):
+        code = codes[0, l * 16 + start + u]
+        real = code < limit
+        slot = jnp.clip(jnp.where(real, code, spare) % STAGE, 0, held.shape[0] - 1)
+        rows.append(jnp.concatenate((held[slot, :LEAF, :], side[slot]), axis=1))
+        flag = jnp.where(real, 1.0, 0.0)
+        weights.append((unpacked(held[slot, LEAF:, :]).astype(F32) * flag).astype(BF16))
+    return weighted(jnp.concatenate(rows, axis=0), jnp.concatenate(weights, axis=1), target)
+
+
 def exchange_kernel(
     points, charges, near, near_smem, interp_hbm, skel_leaf, mid_hbm, skel_mid, partners, top, skel_top,
-    recv, total, targets,
+    recv, total, targets, codes_out,
     interp, interp_mid, lists, list_in, charge_pack, send, own_side, skel_cols,
-    mid_a, mid_b, scatter, scatter_in, gathered, crossed,
+    mid_a, mid_b, scatter, scatter_in, gathered, crossed, early, held, side, codes,
     local_sem, list_s, list_r, near_s, near_r, ma_s, ma_r, mb_s, mb_r, sc_s, sc_r, ga_s, ga_r, cr_s, cr_r,
 ):
     me, group = lax.axis_index("sub"), lax.axis_index("leaf")
@@ -110,13 +164,13 @@
     list_copies = [None] + [
         in_sub(lists, list_in.at[k], list_s.at[k], list_r.at[k], k) for k in range(1, N_SUB)
     ]
-    order = [k for ks in GROUPS for k in ks]
+    order = ORDER
     for k in order:
         list_copies[k].start()
 
     @pl.loop(0, LEAVES)
     def _(l):
-        charge_pack[l] = packed(jnp.transpose(charges[l]))
+        charge_pack[l] = packed(charges[:, pl.ds(pl.multiple_of(l * LEAF, LEAF), LEAF)])
 
     steps = [(ks, s) for ks in GROUPS for s in range(2)]
     near_copies = []
@@ -144,13 +198,24 @@
             leaf = chosen[k][s]
             send[k, s, :LEAF, :] = points[leaf]
             send[k, s, LEAF:, :] = charge_pack[leaf]
-            c = in_sub(send.at[k, s], recv.at[k, s], near_s.at[k, s], near_r.at[k, s], k)
+            at = 2 * ORDER.index(k) + s
+            if at < 2 * EARLY:
+                landing = early.at[at]
+            elif at < 2 * MIDDLE:
+                landing = held.at[at]
+            else:
+                landing = recv.at[at]
+            c = in_sub(send.at[k, s], landing, near_s.at[k, s], near_r.at[k, s], k)
             c.start()
             started.append(c)
         near_copies.append(started)
 
     for _ in range(WINDOW):
         advance()
+
+    codes_out[...] = jnp.broadcast_to(sorted_lists(lists, group * N_SUB * LEAVES, z, y), codes_out.shape)
+    save_codes = pltpu.make_async_copy(codes_out, codes, local_sem.at[2])
+    save_codes.start()
 
     load_interp.wait()
     load_mid.wait()
@@ -225,6 +290,8 @@
 
     own_chunk(0, 2)
     advance()
+    own_chunk(2, 4)
+    advance()
 
     for pair in first:
         for c in pair:
@@ -235,7 +302,6 @@
                        in_sub(mid_b.at[0], mid_b.at[d], mb_s.at[1, d], mb_r.at[1, d], d)))
         for c in second[-1]:
             c.start()
-    advance()
 
     for c in scatter_copies:
         c.wait_recv()
@@ -249,21 +315,46 @@
         c.start()
         gather_copies.append(c)
 
-    own_chunk(2, 4)
     advance()
     own_chunk(4, 6)
     advance()
-
-    for c in gather_copies:
-        c.wait_recv()
-    cross_copies = []
-    for j in (1, 7, 2, 6, 3, 5, 4):
-        c = remote(gathered, crossed.at[j - 1], cr_s.at[j - 1], cr_r.at[j - 1], ((group + j) % N_LEAF, me))
-        c.start()
-        cross_copies.append(c)
     own_chunk(6, 8)
     advance()
-    advance()
+
+    save_codes.wait()
+
+    def arrived(begin, end):
+        for ks, copies in zip([g for g in GROUPS for _ in range(2)], near_copies):
+            for k, c in zip(ks, copies):
+                if begin <= ORDER.index(k) < end:
+                    c.wait_recv()
+
+    arrived(0, EARLY)
+    keep_early = pltpu.make_async_copy(early, held.at[pl.ds(0, 2 * EARLY)], local_sem.at[3])
+    keep_early.start()
+
+    @pl.loop(0, 2 * EARLY)
+    def _(i):
+        side[i] = source_side(early[i, :LEAF, :])
+
+    advance()
+
+    def first_pass(l):
+        total[l] += listed_pairs(codes, l, 0, STAGE, early, side, targets[l])
+
+    for begin in range(0, LEAVES, 2):
+        pl.loop(begin, begin + 2)(first_pass)
+        advance()
+        if begin == 2:
+            for c in gather_copies:
+                c.wait_recv()
+            cross_copies = []
+            for j in (1, 7, 2, 6, 3, 5, 4):
+                c = remote(gathered, crossed.at[j - 1], cr_s.at[j - 1], cr_r.at[j - 1], ((group + j) % N_LEAF, me))
+                c.start()
+                cross_copies.append(c)
+    while len(near_copies) < len(steps):
+        advance()
 
     for pair in second:
         for c in pair:
@@ -277,7 +368,20 @@
         rows.append(jnp.concatenate((block[:SKEL], source_side(block[:SKEL])), axis=1))
         weights.append(unpacked(block[SKEL:]))
     mid_sum = weighted(jnp.concatenate(rows, axis=0), jnp.concatenate(weights, axis=1), mid_targets)
-    advance()
+
+    keep_early.wait()
+    arrived(EARLY, MIDDLE)
+    keep_held = pltpu.make_async_copy(held, recv.at[pl.ds(0, 2 * MIDDLE)], local_sem.at[4])
+    keep_held.start()
+
+    @pl.loop(2 * EARLY, 2 * MIDDLE)
+    def _(i):
+        side[i] = source_side(held[i, :LEAF, :])
+
+    @pl.loop(0, LEAVES)
+    def _(l):
+        start, _, _ = progress(codes, l)
+        total[l] += listed_pairs(codes, l, start, 2 * STAGE, held, side, targets[l])
 
     for c in cross_copies:
         c.wait_recv()
@@ -290,81 +394,60 @@
 
     top_sum = lax.fori_loop(0, N_LEAF - 1, top_from, jnp.zeros((RHS, SKEL), F32)).astype(BF16)
     mid_total = (mid_sum + dot_nt(top_sum, top[...])).astype(BF16)
-    advance()
 
     @pl.loop(0, LEAVES)
     def _(l):
         down = dot_nt(mid_total, interp_mid[pl.ds(pl.multiple_of(l * SKEL, SKEL), SKEL), :]).astype(BF16)
         total[l] += dot_nt(down, interp[l])
 
-    while len(near_copies) < len(steps):
-        advance()
     for t, copies in enumerate(near_copies):
         for c in copies:
             if t >= len(steps) - WINDOW:
                 c.wait_send()
-            c.wait_recv()
     for c in list_copies[1:] + scatter_copies + gather_copies + cross_copies:
         c.wait_send()
     for pair in first + second:
         for c in pair:
             c.wait_send()
-
-
-def near_kernel(near, recv, targets, total, out, side, listed, count, lowest, used):
-    me, group = lax.axis_index("sub"), lax.axis_index("leaf")
-    z, y = me // 4, me % 4
-    base = group * N_SUB * LEAVES
-
-    for i in range(N_SUB):
-        lowest[i] = LEAVES
-    for i in range(2 * N_SUB):
+    keep_held.wait()
+    arrived(MIDDLE, N_SUB)
+
+
+def near_kernel(codes, recv, targets, total, out, held, side, used, sem):
+    slots = held.shape[0]
+    for i in range(STAGE):
         used[i] = 0
 
     @pl.loop(0, LEAVES)
     def _(l):
-        for e in range(1, NEAR):
-            named = near[l, e] - base
-            owner, leaf = named // LEAVES, named % LEAVES
-            lowest[owner] = jnp.minimum(lowest[owner], leaf)
-
-    @pl.loop(0, LEAVES)
-    def _(l):
-        held = jnp.int32(0)
-        for e in range(1, NEAR):
-            named = near[l, e] - base
-            owner, leaf = named // LEAVES, named % LEAVES
-            shift = ((z + 4 - owner // 4) % 4) * 4 + (y + 4 - owner % 4) % 4
-            slot = 2 * shift + jnp.where(leaf == lowest[owner], 0, 1)
-            listed[l, held] = slot
-            there = jnp.where(owner == me, 0, 1)
-            used[slot] = jnp.maximum(used[slot], there)
-            held = held + there
-        count[l] = held
-
-    @pl.loop(2, 2 * N_SUB)
+        _, begin, end = progress(codes, l)
+        for e in range(NEAR):
+            slot = codes[0, l * 16 + e] % STAGE
+            used[slot] = jnp.maximum(used[slot], jnp.where((begin <= e) & (e < end), 1, 0))
+
+    def copy(i):
+        return pltpu.make_async_copy(recv.at[i], held.at[i], sem.at[i])
+
+    @pl.loop(0, slots)
+    def _(i):
+        pl.when(used[i] > 0)(lambda: copy(i).start())
+
+    @pl.loop(0, slots)
     def _(i):
         @pl.when(used[i] > 0)
         def _():
-            side[i] = source_side(recv[i, :LEAF, :])
+            copy(i).wait()
+            side[i] = source_side(held[i, :LEAF, :])
 
     @pl.loop(0, LEAVES)
     def _(l):
-        held = count[l]
+        _, begin, end = progress(codes, l)
 
         def four(n, acc):
-            rows, weights = [], []
-            for u in range(4):
-                e = n * 4 + u
-                real = e < held
-                slot = listed[l, jnp.where(real, e, 0)]
-                rows.append(jnp.concatenate((recv[slot, :LEAF, :], side[slot]), axis=1))
-                flag = jnp.where(real, 1.0, 0.0)
-                weights.append((unpacked(recv[slot, LEAF:, :]).astype(F32) * flag).astype(BF16))
-            return acc + weighted(jnp.concatenate(rows, axis=0), jnp.concatenate(weights, axis=1), targets[l])
-
-        acc = lax.fori_loop(0, (held + 3) // 4, four, total[l])
-        out[l] = jnp.transpose(acc)
+            return acc + listed_pairs(codes, l, begin + 4 * n, 3 * STAGE, held, side, targets[l])
+
+        acc = lax.fori_loop(0, (end - begin + 3) // 4, four, total[l])
+        out[:, pl.ds(pl.multiple_of(l * LEAF, LEAF), LEAF)] = acc
 
 
 def body(
@@ -373,15 +456,17 @@
 ):
     vmem, smem, hbm = (pl.BlockSpec(memory_space=m) for m in (pltpu.VMEM, pltpu.SMEM, pl.ANY))
     dma = pltpu.SemaphoreType.DMA
-    recv, total, targets = pl.pallas_call(
+    slots = 2 * (N_SUB - 1)
+    recv, total, targets, codes = pl.pallas_call(
         exchange_kernel,
         out_shape=(
-            jax.ShapeDtypeStruct((N_SUB, 2, SLOT, DIM), BF16),
+            jax.ShapeDtypeStruct((slots, SLOT, DIM), BF16),
             jax.ShapeDtypeStruct((LEAVES, RHS, LEAF), F32),
             jax.ShapeDtypeStruct((LEAVES, 2 * DIM, LEAF), BF16),
+            jax.ShapeDtypeStruct((8, 128), I32),
         ),
         in_specs=[vmem, vmem, vmem, smem, hbm, vmem, hbm, vmem, smem, vmem, vmem],
-        out_specs=(hbm, vmem, vmem),
+        out_specs=(hbm, vmem, vmem, vmem),
         scratch_shapes=[
             pltpu.VMEM((LEAVES, LEAF, SKEL), BF16),
             pltpu.VMEM((LEAVES * SKEL, SKEL), BF16),
@@ -397,7 +482,11 @@
             pltpu.VMEM((N_SUB, SKEL // N_SUB, 2 * DIM), F32),
             pltpu.VMEM((SKEL, 2 * DIM), BF16),
             pltpu.VMEM((N_LEAF - 1, SKEL, 2 * DIM), BF16),
-            dma((2,)),
+            pltpu.VMEM((2 * EARLY, SLOT, DIM), BF16),
+            pltpu.VMEM((2 * MIDDLE, SLOT, DIM), BF16),
+            pltpu.VMEM((2 * MIDDLE, LEAF, DIM), BF16),
+            pltpu.SMEM((8, 128), I32),
+            dma((5,)),
             dma((N_SUB,)), dma((N_SUB,)),
             dma((N_SUB, 2)), dma((N_SUB, 2)),
             dma((2, 4)), dma((2, 4)), dma((2, 4)), dma((2, 4)),
@@ -409,24 +498,23 @@
             collective_id=0, has_side_effects=True, vmem_limit_bytes=56 << 20
         ),
     )(
-        points.reshape(LEAVES, LEAF, DIM), charges.reshape(LEAVES, LEAF, RHS), near_leaves, near_leaves,
+        points.reshape(LEAVES, LEAF, DIM), charges.T, near_leaves, near_leaves,
         leaf_interpolant, skel_leaf, interp_mid[0], skel_mid, mid_partners, interp_top[0], skel_top,
     )
     out = pl.pallas_call(
         near_kernel,
-        out_shape=jax.ShapeDtypeStruct((LEAVES, LEAF, RHS), F32),
-        in_specs=[smem, vmem, vmem, vmem],
+        out_shape=jax.ShapeDtypeStruct((RHS, LEAVES * LEAF), F32),
+        in_specs=[smem, hbm, vmem, vmem],
         out_specs=vmem,
         scratch_shapes=[
-            pltpu.VMEM((2 * N_SUB, LEAF, DIM), BF16),
-            pltpu.SMEM((LEAVES, 16), I32),
-            pltpu.SMEM((LEAVES,), I32),
-            pltpu.SMEM((N_SUB,), I32),
-            pltpu.SMEM((2 * N_SUB,), I32),
+            pltpu.VMEM((slots, SLOT, DIM), BF16),
+            pltpu.VMEM((slots, LEAF, DIM), BF16),
+            pltpu.SMEM((STAGE,), I32),
+            dma((slots,)),
         ],
         compiler_params=pltpu.CompilerParams(vmem_limit_bytes=56 << 20),
-    )(near_leaves, recv.reshape(2 * N_SUB, SLOT, DIM), targets, total)
-    return out.reshape(LEAVES * LEAF, RHS)
+    )(codes, recv, targets, total)
+    return out.T
 
 
 def solution(mesh):

time: 158 us -> 134 us (0.85)
  the two profiles are of different devices: /device:TPU:12 before, /device:TPU:124 now
where the time goes in v2:
time: 134 us; the launch traced here: 133 us
  Pallas kernels  133 us (99%)
    pallas_call x1, Pallas kernels, body(): pl.pallas_call(exchange_kernel, out_shape=(jax.ShapeDtypeStruct((slots, S...  119 us
    pallas_call x1, Pallas kernels, body(): pl.pallas_call(near_kernel, out_shape=jax.ShapeDtypeStruct((RHS, LEAVES *...  14 us

profile of v2, /device:TPU:124, one launch (start us, length us, event | category | flops | bytes accessed | tf_op | source)
XLA Modules:
  0.0 133.4 jit_solution(1525908208516967304)
XLA Ops:
  0.0 119.2 %shard_map.100 = (bf16[30,768,128]{2,1,0:T(8,128)(2,1)}, f32[8,64,512]{2,1,0:T(8,128)}, bf16[8,256,512]{2,1,0:T(8,128)(2,1)}, s32[8,128]{1,0:T(8,128)}) custom-call(bf16[8,512,128]{2,1,0:T(8,128)(2,1)} %bitcast.5, bf16[64,4096]{1,0:T(8,128)(2,1)} %bitcast.7, s32[8,12]{1,0:T(8,128)} %near_smem.1, s32[8,12]{1,0:T(8,128)} %near_smem.1, ...), custom_call_target="tpu_custom_call" | custom-call | tf_op jit(solution)/shard_map/pallas_call | solution.py:460
  119.3 14.0 %shard_map.101 = f32[64,4096]{1,0:T(8,128)} custom-call(s32[8,128]{1,0:T(8,128)} %get-tuple-element.9.codes, bf16[30,768,128]{2,1,0:T(8,128)(2,1)} %get-tuple-element.10.recv, bf16[8,256,512]{2,1,0:T(8,128)(2,1)} %get-tuple-element.11.targets, f32[8,64,512]{2,1,0:T(8,128)} %get-tuple-element.12.total), custom_call_target="tpu_custom_call" | custom-call | tf_op jit(solution)/shard_map/pallas_call | solution.py:504

commit v3 on v2

--- a/solution.py
+++ b/solution.py
@@ -20,7 +20,7 @@
 GROUPS = ((6, 12), (4, 14), (9, 3), (1, 11), (10,), (5, 15), (7, 13), (2, 8))
 WINDOW = 5
 ORDER = [k for ks in GROUPS for k in ks]
-EARLY, MIDDLE = 8, 11
+EARLY, MIDDLE = 8, 13
 STAGE = 64
 
 
@@ -112,10 +112,10 @@
     return first, first + jnp.minimum(both - first, 4), remote
 
 
-def listed_pairs(codes, l, start, limit, held, side, target):
+def listed_pairs(codes, l, start, width, limit, held, side, target):
     rows, weights = [], []
     spare = jnp.where(codes[0, l * 16 + start] < limit, codes[0, l * 16 + start], 0)
-    for u in range(4):
+    for u in range(width):
         code = codes[0, l * 16 + start + u]
         real = code < limit
         slot = jnp.clip(jnp.where(real, code, spare) % STAGE, 0, held.shape[0] - 1)
@@ -172,18 +172,10 @@
     def _(l):
         charge_pack[l] = packed(charges[:, pl.ds(pl.multiple_of(l * LEAF, LEAF), LEAF)])
 
-    steps = [(ks, s) for ks in GROUPS for s in range(2)]
-    near_copies = []
     chosen = {}
-
-    def advance():
-        t = len(near_copies)
-        if t >= len(steps):
-            return
-        if t >= WINDOW:
-            for c in near_copies[t - WINDOW]:
-                c.wait_send()
-        ks, s = steps[t]
+    arrivals = {}
+
+    def near_step(ks, s):
         started = []
         for k in ks:
             if s == 0:
@@ -208,7 +200,37 @@
             c = in_sub(send.at[k, s], landing, near_s.at[k, s], near_r.at[k, s], k)
             c.start()
             started.append(c)
-        near_copies.append(started)
+            arrivals[at] = c
+        return started
+
+    first, second = [], []
+
+    def mid_step(ds):
+        started = []
+        for d in ds:
+            started += [in_sub(mid_a.at[0], mid_a.at[d], ma_s.at[1, d], ma_r.at[1, d], 4 * d),
+                        in_sub(mid_b.at[0], mid_b.at[d], mb_s.at[1, d], mb_r.at[1, d], d)]
+        if not second:
+            for c in first:
+                c.wait_recv()
+        for c in started:
+            c.start()
+        second.extend(started)
+        return started
+
+    steps = [(near_step, (ks, s)) for ks in GROUPS for s in range(2)]
+    steps[10:10] = [(mid_step, ((1, 3),)), (mid_step, ((2,),))]
+    taken = []
+
+    def advance():
+        t = len(taken)
+        if t >= len(steps):
+            return
+        if t >= WINDOW:
+            for c in taken[t - WINDOW]:
+                c.wait_send()
+        step, args = steps[t]
+        taken.append(step(*args))
 
     for _ in range(WINDOW):
         advance()
@@ -243,12 +265,11 @@
     own_mid = jnp.concatenate((mid_rows, packed(mid_up)), axis=0)
     mid_a[0, 0] = own_mid[:HALF]
     mid_b[0, 0] = own_mid[HALF:]
-    first = []
     for d in (1, 3, 2):
-        first.append((in_sub(mid_a.at[0, 0], mid_a.at[0, d], ma_s.at[0, d], ma_r.at[0, d], d),
-                      in_sub(mid_b.at[0, 0], mid_b.at[0, d], mb_s.at[0, d], mb_r.at[0, d], 4 * d)))
-        for c in first[-1]:
-            c.start()
+        first.append(in_sub(mid_a.at[0, 0], mid_a.at[0, d], ma_s.at[0, d], ma_r.at[0, d], d))
+        first.append(in_sub(mid_b.at[0, 0], mid_b.at[0, d], mb_s.at[0, d], mb_r.at[0, d], 4 * d))
+    for c in first:
+        c.start()
 
     row = lax.broadcasted_iota(I32, (SKEL, SKEL), 0) + me * SKEL
     picks = jnp.where(row == skel_top[...], 1.0, 0.0).astype(BF16)
@@ -293,16 +314,6 @@
     own_chunk(2, 4)
     advance()
 
-    for pair in first:
-        for c in pair:
-            c.wait_recv()
-    second = []
-    for d in (1, 3, 2):
-        second.append((in_sub(mid_a.at[0], mid_a.at[d], ma_s.at[1, d], ma_r.at[1, d], 4 * d),
-                       in_sub(mid_b.at[0], mid_b.at[d], mb_s.at[1, d], mb_r.at[1, d], d)))
-        for c in second[-1]:
-            c.start()
-
     for c in scatter_copies:
         c.wait_recv()
     summed = scatter[rows_of(me), :]
@@ -324,10 +335,8 @@
     save_codes.wait()
 
     def arrived(begin, end):
-        for ks, copies in zip([g for g in GROUPS for _ in range(2)], near_copies):
-            for k, c in zip(ks, copies):
-                if begin <= ORDER.index(k) < end:
-                    c.wait_recv()
+        for at in range(2 * begin, 2 * end):
+            arrivals[at].wait_recv()
 
     arrived(0, EARLY)
     keep_early = pltpu.make_async_copy(early, held.at[pl.ds(0, 2 * EARLY)], local_sem.at[3])
@@ -340,7 +349,7 @@
     advance()
 
     def first_pass(l):
-        total[l] += listed_pairs(codes, l, 0, STAGE, early, side, targets[l])
+        total[l] += listed_pairs(codes, l, 0, 4, STAGE, early, side, targets[l])
 
     for begin in range(0, LEAVES, 2):
         pl.loop(begin, begin + 2)(first_pass)
@@ -353,12 +362,11 @@
                 c = remote(gathered, crossed.at[j - 1], cr_s.at[j - 1], cr_r.at[j - 1], ((group + j) % N_LEAF, me))
                 c.start()
                 cross_copies.append(c)
-    while len(near_copies) < len(steps):
+    while len(taken) < len(steps):
         advance()
 
-    for pair in second:
-        for c in pair:
-            c.wait_recv()
+    for c in second:
+        c.wait_recv()
     mid_targets = target_side(mid_cols.astype(BF16))
     rows, weights = [], []
     for p in range(4):
@@ -369,6 +377,23 @@
         weights.append(unpacked(block[SKEL:]))
     mid_sum = weighted(jnp.concatenate(rows, axis=0), jnp.concatenate(weights, axis=1), mid_targets)
 
+    for c in cross_copies:
+        c.wait_recv()
+    top_targets = target_side(jnp.transpose(gathered[:, DIM:].astype(F32)).astype(BF16))
+
+    def top_from(j, acc):
+        rows = crossed[j, :, DIM:]
+        weights = jnp.transpose(crossed[j, :, :DIM].astype(F32)).astype(BF16)[:RHS]
+        return acc + weighted(jnp.concatenate((rows, source_side(rows)), axis=1), weights, top_targets)
+
+    top_sum = lax.fori_loop(0, N_LEAF - 1, top_from, jnp.zeros((RHS, SKEL), F32)).astype(BF16)
+    mid_total = (mid_sum + dot_nt(top_sum, top[...])).astype(BF16)
+
+    @pl.loop(0, LEAVES)
+    def _(l):
+        down = dot_nt(mid_total, interp_mid[pl.ds(pl.multiple_of(l * SKEL, SKEL), SKEL), :]).astype(BF16)
+        total[l] += dot_nt(down, interp[l])
+
     keep_early.wait()
     arrived(EARLY, MIDDLE)
     keep_held = pltpu.make_async_copy(held, recv.at[pl.ds(0, 2 * MIDDLE)], local_sem.at[4])
@@ -381,36 +406,15 @@
     @pl.loop(0, LEAVES)
     def _(l):
         start, _, _ = progress(codes, l)
-        total[l] += listed_pairs(codes, l, start, 2 * STAGE, held, side, targets[l])
-
-    for c in cross_copies:
-        c.wait_recv()
-    top_targets = target_side(jnp.transpose(gathered[:, DIM:].astype(F32)).astype(BF16))
-
-    def top_from(j, acc):
-        rows = crossed[j, :, DIM:]
-        weights = jnp.transpose(crossed[j, :, :DIM].astype(F32)).astype(BF16)[:RHS]
-        return acc + weighted(jnp.concatenate((rows, source_side(rows)), axis=1), weights, top_targets)
-
-    top_sum = lax.fori_loop(0, N_LEAF - 1, top_from, jnp.zeros((RHS, SKEL), F32)).astype(BF16)
-    mid_total = (mid_sum + dot_nt(top_sum, top[...])).astype(BF16)
-
-    @pl.loop(0, LEAVES)
-    def _(l):
-        down = dot_nt(mid_total, interp_mid[pl.ds(pl.multiple_of(l * SKEL, SKEL), SKEL), :]).astype(BF16)
-        total[l] += dot_nt(down, interp[l])
-
-    for t, copies in enumerate(near_copies):
+        total[l] += listed_pairs(codes, l, start, 4, 2 * STAGE, held, side, targets[l])
+
+    for copies in taken[len(steps) - WINDOW :]:
         for c in copies:
-            if t >= len(steps) - WINDOW:
-                c.wait_send()
-    for c in list_copies[1:] + scatter_copies + gather_copies + cross_copies:
+            c.wait_send()
+    for c in list_copies[1:] + first + scatter_copies + gather_copies + cross_copies:
         c.wait_send()
-    for pair in first + second:
-        for c in pair:
-            c.wait_send()
     keep_held.wait()
-    arrived(MIDDLE, N_SUB)
+    arrived(MIDDLE, N_SUB - 1)
 
 
 def near_kernel(codes, recv, targets, total, out, held, side, used, sem):
@@ -443,10 +447,10 @@
     def _(l):
         _, begin, end = progress(codes, l)
 
-        def four(n, acc):
-            return acc + listed_pairs(codes, l, begin + 4 * n, 3 * STAGE, held, side, targets[l])
-
-        acc = lax.fori_loop(0, (end - begin + 3) // 4, four, total[l])
+        def two(n, acc):
+            return acc + listed_pairs(codes, l, begin + 2 * n, 2, 3 * STAGE, held, side, targets[l])
+
+        acc = lax.fori_loop(0, (end - begin + 1) // 2, two, total[l])
         out[:, pl.ds(pl.multiple_of(l * LEAF, LEAF), LEAF)] = acc
 
 

time: 134 us -> 133 us (level)
  the two profiles are of different devices: /device:TPU:124 before, /device:TPU:2 now
where the time goes in v3:
time: 133 us
  Pallas kernels  132 us (99%)
    pallas_call x1, Pallas kernels, body(): pl.pallas_call(exchange_kernel, out_shape=(jax.ShapeDtypeStruct((slots, S...  119 us
    pallas_call x1, Pallas kernels, body(): pl.pallas_call(near_kernel, out_shape=jax.ShapeDtypeStruct((RHS, LEAVES *...  13 us

profile of v3, /device:TPU:2, one launch (start us, length us, event | category | flops | bytes accessed | tf_op | source)
XLA Modules:
  0.0 132.6 jit_solution(18067297659048221770)
XLA Ops:
  0.0 119.4 %shard_map.100 = (bf16[30,768,128]{2,1,0:T(8,128)(2,1)}, f32[8,64,512]{2,1,0:T(8,128)}, bf16[8,256,512]{2,1,0:T(8,128)(2,1)}, s32[8,128]{1,0:T(8,128)}) custom-call(bf16[8,512,128]{2,1,0:T(8,128)(2,1)} %bitcast.5, bf16[64,4096]{1,0:T(8,128)(2,1)} %bitcast.7, s32[8,12]{1,0:T(8,128)} %near_smem.1, s32[8,12]{1,0:T(8,128)} %near_smem.1, ...), custom_call_target="tpu_custom_call" | custom-call | tf_op jit(solution)/shard_map/pallas_call | solution.py:464
  119.4 13.0 %shard_map.101 = f32[64,4096]{1,0:T(8,128)} custom-call(s32[8,128]{1,0:T(8,128)} %get-tuple-element.9.codes, bf16[30,768,128]{2,1,0:T(8,128)(2,1)} %get-tuple-element.10.recv, bf16[8,256,512]{2,1,0:T(8,128)(2,1)} %get-tuple-element.11.targets, f32[8,64,512]{2,1,0:T(8,128)} %get-tuple-element.12.total), custom_call_target="tpu_custom_call" | custom-call | tf_op jit(solution)/shard_map/pallas_call | solution.py:508

commit v4 on v3

--- a/solution.py
+++ b/solution.py
@@ -20,7 +20,7 @@
 GROUPS = ((6, 12), (4, 14), (9, 3), (1, 11), (10,), (5, 15), (7, 13), (2, 8))
 WINDOW = 5
 ORDER = [k for ks in GROUPS for k in ks]
-EARLY, MIDDLE = 8, 13
+EARLY, MIDDLE = 8, 11
 STAGE = 64
 
 

time: 133 us -> 137 us (1.030)
  Pallas kernels: 132 us -> 137 us
    pallas_call x1, Pallas kernels: 13 us -> 18.6 us  [body(): pl.pallas_call(near_kernel, out_shape=jax.ShapeDtypeStruct((RHS, LEAVES *...]
where the time goes in v4:
time: 137 us
  Pallas kernels  137 us (100%)
    pallas_call x1, Pallas kernels, body(): pl.pallas_call(exchange_kernel, out_shape=(jax.ShapeDtypeStruct((slots, S...  118 us
    pallas_call x1, Pallas kernels, body(): pl.pallas_call(near_kernel, out_shape=jax.ShapeDtypeStruct((RHS, LEAVES *...  18.6 us

profile of v4, /device:TPU:2, one launch (start us, length us, event | category | flops | bytes accessed | tf_op | source)
XLA Modules:
  0.0 137.2 jit_solution(8233802625678751193)
XLA Ops:
  0.0 118.4 %shard_map.100 = (bf16[30,768,128]{2,1,0:T(8,128)(2,1)}, f32[8,64,512]{2,1,0:T(8,128)}, bf16[8,256,512]{2,1,0:T(8,128)(2,1)}, s32[8,128]{1,0:T(8,128)}) custom-call(bf16[8,512,128]{2,1,0:T(8,128)(2,1)} %bitcast.5, bf16[64,4096]{1,0:T(8,128)(2,1)} %bitcast.7, s32[8,12]{1,0:T(8,128)} %near_smem.1, s32[8,12]{1,0:T(8,128)} %near_smem.1, ...), custom_call_target="tpu_custom_call" | custom-call | tf_op jit(solution)/shard_map/pallas_call | solution.py:464
  118.4 18.6 %shard_map.101 = f32[64,4096]{1,0:T(8,128)} custom-call(s32[8,128]{1,0:T(8,128)} %get-tuple-element.9.codes, bf16[30,768,128]{2,1,0:T(8,128)(2,1)} %get-tuple-element.10.recv, bf16[8,256,512]{2,1,0:T(8,128)(2,1)} %get-tuple-element.11.targets, f32[8,64,512]{2,1,0:T(8,128)} %get-tuple-element.12.total), custom_call_target="tpu_custom_call" | custom-call | tf_op jit(solution)/shard_map/pallas_call | solution.py:508
